TPU v7x, 128 devices: a whole 4x4x4 slice. The times are simulated.
128 devices in a mesh: dp: 8 (over x_lo, z), ctx: 16 (over y, x_hi, core).
Axes of the slice: x: 4 (x_hi: 2, x_lo: 2; x = x_hi * 2 + x_lo), y: 4, z: 4, core: 2. Of those that a mesh axis runs over, the one named last changes fastest.
Arguments:
- queries: bfloat16 [8, 2048, 2048], P('dp', 'ctx'), may hold values from -6 to 6
- key_proj: bfloat16 [8, 2048, 2048], P('dp', 'ctx'), may hold values from -6 to 6
- value_proj: bfloat16 [8, 2048, 2048], P('dp', 'ctx'), may hold values from -6 to 6
- filters: float32 [2048, 2048], P(None, 'ctx'), may hold values from -1.2 to 1.2
- out_weight: bfloat16 [2048, 2048], P('ctx'), may hold values from -0.125 to 0.125
- out_grad: bfloat16 [8, 2048, 2048], P('dp', 'ctx'), may hold values from -6 to 6
Outputs:
- block_out: bfloat16 [8, 2048, 2048], P('dp', 'ctx')
- query_grad: bfloat16 [8, 2048, 2048], P('dp', 'ctx')
- key_grad: bfloat16 [8, 2048, 2048], P('dp', 'ctx')
- value_grad: bfloat16 [8, 2048, 2048], P('dp', 'ctx')
- filter_grad: float32 [2048, 2048], P(None, 'ctx')
- weight_grad: float32 [2048, 2048], P('ctx')
All inputs are finite; a program needn't handle non-finite values.
Results may differ from a plain program's by a relative error of at most 0.023.
Values may be sent and summed in bfloat16 or wider, within the bound.
A program may use at most 128 MiB of HBM per device.

v0:
```python
import math

import jax
import jax.numpy as jnp
import ml_dtypes
import numpy as np
from jax import lax
from jax.experimental import pallas as pl
from jax.experimental.pallas import tpu as pltpu
from jax.sharding import PartitionSpec as P

MESH = pl.DeviceIdType.MESH
BF = jnp.bfloat16
F32 = jnp.float32


def make_tables():
    k0 = np.arange(16)
    t1 = np.arange(16)
    angle = 2.0 * np.pi * (k0[:, None] + 0.5) * t1[None, :] / 32.0
    outer = np.stack([np.cos(angle), -np.sin(angle)], axis=1)
    outer = np.einsum("krt,su->krstu", outer, np.eye(16)).reshape(512, 256)
    t0 = np.arange(128)
    k1 = np.arange(128)
    angle = (k0[:, None, None] + 0.5) * t0[None, None, :] / 4096.0 + (
        (k1[None, :, None] * t0[None, None, :]) % 128
    ) / 128.0
    cos = np.cos(2.0 * np.pi * angle).reshape(16, 128, 8, 16)
    sin = np.sin(2.0 * np.pi * angle).reshape(16, 128, 8, 16)
    inner = np.empty((16, 2, 128, 8, 2, 16))
    inner[:, 0, :, :, 0] = cos
    inner[:, 0, :, :, 1] = sin
    inner[:, 1, :, :, 0] = -sin
    inner[:, 1, :, :, 1] = cos
    inner = inner.reshape(16, 256, 256)
    return tuple(
        np.ascontiguousarray(table).astype(ml_dtypes.bfloat16)
        for table in (outer, outer.T, inner, inner.transpose(0, 2, 1))
    )


def dot(a, b):
    return jnp.dot(a, b, preferred_element_type=F32)


def times(a, b, conj):
    ar, ai, br, bi = a[:128], a[128:], b[:128], b[128:]
    if conj:
        return jnp.concatenate([ar * br + ai * bi, ar * bi - ai * br], axis=0)
    return jnp.concatenate([ar * br - ai * bi, ar * bi + ai * br], axis=0)


def loop(n, body, unroll=1):
    def step(at, carry):
        body(at)
        return carry

    lax.fori_loop(0, n, step, 0, unroll=unroll)


def rows16(g):
    return pl.ds(pl.multiple_of(g * 16, 16), 16)


def kernel(
    q_in, k_in, v_in, h_in, w_in, g_in, p1_in, p1t_in, m_in, mt_in,
    block_out, query_out, mixed_out, filter_out, weight_out,
    q_v, k_v, v_v, h_v, p1, p1t, m_t, mt_t,
    mixed_send, mixed_recv, q_send, q_tile, g_tile, w_tile,
    conv_send, conv_tile, gg_tile, cg_send, cg_recv, gated, gated_t,
    qg_send, qg_recv, block_send, block_recv, wg_send, wg_recv,
    mg_send, mg_recv, f_send, f_recv, ws_send, ws_recv,
    s_buf, u_buf, u2_buf, h_spec, m_spec,
    lsem,
    mixed_s, mixed_r, q_s, q_r, g_s, g_r, w_s, w_r, conv_s, conv_r, cg_s, cg_r, qg_s, qg_r,
    block_s, block_r, wg_s, wg_r, mg_s, mg_r, f_s, f_r, fa_s, fa_r, ws_s, ws_r, wa_s, wa_r,
):
    dp = lax.axis_index("dp")
    me = lax.axis_index("ctx")
    i = lax.div(me, 4)
    j = lax.rem(me, 4)

    def ctx_peer(at):
        return lax.rem(me + at, 16)

    def dp_peer(at):
        return lax.rem(dp + at, 8)

    def i_peer(at):
        return lax.rem(i + at, 4)

    def j_peer(at):
        return lax.rem(j + at, 4)

    def remote(src, dst, s, r, to_dp, to_ctx):
        return pltpu.make_async_remote_copy(
            src_ref=src, dst_ref=dst, send_sem=s, recv_sem=r,
            device_id=(to_dp, to_ctx), device_id_type=MESH,
        )

    def mixed_copy(at):
        p = ctx_peer(at)
        return remote(mixed_send.at[p], mixed_recv.at[me], mixed_s.at[at], mixed_r.at[at], dp, p)

    def mg_copy(at):
        p = ctx_peer(at)
        return remote(mg_send.at[p], mg_recv.at[me], mg_s.at[at], mg_r.at[at], dp, p)

    def q_copy(at):
        p = j_peer(at)
        return remote(q_send.at[p], q_tile.at[:, j], q_s.at[at], q_r.at[at], dp, i * 4 + p)

    def g_copy(at):
        return remote(g_in, g_tile.at[j], g_s.at[at], g_r.at[at], dp, i * 4 + j_peer(at))

    def w_copy(at):
        return remote(w_in, w_tile.at[i], w_s.at[at], w_r.at[at], dp, i_peer(at) * 4 + j)

    def conv_copy(at):
        p = i_peer(at)
        return remote(
            conv_send.at[pl.ds(p * 4, 4)], conv_tile.at[i], conv_s.at[at], conv_r.at[at],
            dp, p * 4 + j,
        )

    def cg_copy(at):
        p = i_peer(at)
        return remote(
            cg_send.at[p], cg_recv.at[pl.ds(i * 4, 4)], cg_s.at[at], cg_r.at[at], dp, p * 4 + j
        )

    def qg_copy(at):
        p = j_peer(at)
        return remote(qg_send.at[p], qg_recv.at[j], qg_s.at[at], qg_r.at[at], dp, i * 4 + p)

    def block_copy(at):
        p = j_peer(at)
        return remote(
            block_send.at[p], block_recv.at[at], block_s.at[at], block_r.at[at], dp, i * 4 + p
        )

    def wg_copy(at):
        p = i_peer(at)
        return remote(wg_send.at[p], wg_recv.at[at], wg_s.at[at], wg_r.at[at], dp, p * 4 + j)

    def f_copy(at):
        p = dp_peer(at)
        return remote(f_send.at[p], f_recv.at[at], f_s.at[at], f_r.at[at], p, me)

    def fa_copy(at):
        p = dp_peer(at)
        return remote(filter_out.at[dp], filter_out.at[dp], fa_s.at[at], fa_r.at[at], p, me)

    def ws_copy(at):
        p = dp_peer(at)
        return remote(ws_send.at[p], ws_recv.at[at], ws_s.at[at], ws_r.at[at], p, me)

    def wa_copy(at):
        p = dp_peer(at)
        return remote(weight_out.at[dp], weight_out.at[dp], wa_s.at[at], wa_r.at[at], p, me)

    def each(copy, n, what):
        loop(n - 1, lambda at: getattr(copy(at + 1), what)())

    local = [
        pltpu.make_async_copy(src, dst, lsem.at[at])
        for at, (src, dst) in enumerate(
            [
                (k_in, k_v), (v_in, v_v), (q_in, q_v), (h_in, h_v), (p1_in, p1), (m_in, m_t),
                (mt_in, mt_t), (p1t_in, p1t), (g_in, g_tile.at[j]), (w_in, w_tile.at[i]),
            ]
        )
    ]
    for copy in local:
        copy.start()

    barrier = pltpu.get_barrier_semaphore()

    def greet_ctx(at):
        pl.semaphore_signal(
            barrier, inc=1, device_id=(dp, ctx_peer(at + 1)), device_id_type=MESH
        )

    def greet_dp(at):
        pl.semaphore_signal(barrier, inc=1, device_id=(dp_peer(at + 1), me), device_id_type=MESH)

    loop(15, greet_ctx)
    loop(7, greet_dp)

    local[0].wait()
    local[1].wait()
    for p in range(16):
        lanes = slice(p * 128, p * 128 + 128)
        mixed_send[p] = (k_v[:, lanes].astype(F32) * v_v[:, lanes].astype(F32)).astype(BF)
    local[2].wait()
    for p in range(16):
        q_send[p % 4, p // 4] = q_v[:, p * 128 : p * 128 + 128]

    pl.semaphore_wait(barrier, 22)
    each(mixed_copy, 16, "start")
    each(q_copy, 4, "start")
    each(w_copy, 4, "start")
    each(g_copy, 4, "start")
    mixed_recv[me] = mixed_send[me]
    q_tile[:, j] = q_send[j]

    def outer_step(x_ref):
        def body(g):
            x = x_ref[:, rows16(g), :].astype(BF).reshape(256, 128)
            s_buf[:, g] = dot(p1[...], x).reshape(16, 32, 128).astype(BF)

        loop(8, body, 2)

    def inner(k0):
        return dot(m_t[k0], s_buf[k0].reshape(256, 128))

    for at in range(3, 8):
        local[at].wait()
    outer_step(h_v)

    def filter_step(k0):
        h_spec[k0] = inner(k0)

    loop(16, filter_step, 2)

    each(mixed_copy, 16, "wait_recv")
    outer_step(mixed_recv)

    def conv_step(k0):
        spec = inner(k0)
        m_spec[k0] = spec
        y = times(h_spec[k0], spec, False).astype(BF)
        u_buf[k0] = dot(mt_t[k0], y).reshape(8, 32, 128).astype(BF)

    loop(16, conv_step, 4)

    def conv_last(g):
        y = dot(p1t[...], u_buf[:, g].reshape(512, 128)) * (1.0 / 2048.0)
        conv_send[:, rows16(g), :] = y.reshape(16, 16, 128).astype(BF)

    loop(8, conv_last, 2)
    each(conv_copy, 4, "start")
    conv_tile[i] = conv_send[pl.ds(i * 4, 4)]

    local[8].wait()
    local[9].wait()
    each(q_copy, 4, "wait_recv")
    each(w_copy, 4, "wait_recv")
    each(g_copy, 4, "wait_recv")
    for half in range(2):
        wide = lax.dot_general(
            g_tile[...].reshape(512, 2048),
            w_tile[2 * half : 2 * half + 2].reshape(256, 2048),
            (((1,), (1,)), ((), ())),
            preferred_element_type=F32,
        ).astype(BF)
        for at in range(2):
            part = 2 * half + at
            gg = wide[:, at * 128 : at * 128 + 128].reshape(4, 128, 128)
            gg_tile[part] = gg
            cg_send[part] = (gg.astype(F32) * q_tile[part].astype(F32)).astype(BF)
    each(cg_copy, 4, "start")
    cg_recv[pl.ds(i * 4, 4)] = cg_send[i]

    each(conv_copy, 4, "wait_recv")
    for part in range(4):
        conv = conv_tile[part].astype(F32)
        gate = (conv * q_tile[part].astype(F32)).astype(BF).reshape(512, 128)
        gated[:, part * 128 : part * 128 + 128] = gate
        gated_t[part * 128 : part * 128 + 128, :] = gate.astype(F32).T.astype(BF)
        qg = (conv * gg_tile[part].astype(F32)).astype(BF)
        for at in range(4):
            qg_send[at, part] = qg[at]
    each(qg_copy, 4, "start")
    qg_recv[j] = qg_send[j]

    def wg_step(n):
        lanes = pl.ds(pl.multiple_of(n * 256, 256), 256)
        y = dot(gated_t[...], g_tile[:, :, lanes].reshape(512, 256))
        wg_send[:, :, lanes] = y.astype(BF).reshape(4, 128, 256)

    loop(8, wg_step)
    each(wg_copy, 4, "start")

    def block_step(n):
        lanes = pl.ds(pl.multiple_of(n * 256, 256), 256)
        y = dot(gated[...], w_tile[:, :, lanes].reshape(512, 256))
        block_send[:, :, lanes] = y.astype(BF).reshape(4, 128, 256)

    loop(8, block_step)
    each(block_copy, 4, "start")

    each(cg_copy, 4, "wait_recv")
    outer_step(cg_recv)

    def back_step(k0):
        spec = inner(k0)
        y = jnp.concatenate(
            [times(h_spec[k0], spec, True), times(m_spec[k0], spec, True)], axis=1
        ).astype(BF)
        u2_buf[k0] = dot(mt_t[k0], y).reshape(8, 32, 256).astype(BF)

    loop(16, back_step, 4)

    def back_last(g):
        y = dot(p1t[...], u2_buf[:, g].reshape(512, 256)) * (1.0 / 2048.0)
        y = y.reshape(16, 16, 256).astype(BF)
        mg_send[:, rows16(g), :] = y[:, :, :128]
        f_send[:, :, rows16(g), :] = y[:, :, 128:].reshape(8, 2, 16, 128)

    loop(8, back_last, 2)
    each(mg_copy, 16, "start")
    each(f_copy, 8, "start")
    mg_recv[me] = mg_send[me]

    each(qg_copy, 4, "wait_recv")
    for p in range(16):
        query_out[:, p * 128 : p * 128 + 128] = qg_recv[p % 4, p // 4]

    each(wg_copy, 4, "wait_recv")

    def wsum_step(r):
        total = wg_send[i, rows16(r), :].astype(F32)
        for at in range(1, 4):
            total += wg_recv[at, rows16(r), :].astype(F32)
        ws_send[r] = total.astype(BF)

    loop(8, wsum_step)
    each(ws_copy, 8, "start")

    each(f_copy, 8, "wait_recv")
    total = f_send[dp].astype(F32)
    for at in range(1, 8):
        total += f_recv[at].astype(F32)
    filter_out[dp] = total.astype(BF)
    each(fa_copy, 8, "start")

    each(block_copy, 4, "wait_recv")

    def bsum_step(r):
        total = block_send[j, rows16(r), :].astype(F32)
        for at in range(1, 4):
            total += block_recv[at, rows16(r), :].astype(F32)
        block_out[rows16(r), :] = total.astype(BF)

    loop(8, bsum_step)

    each(ws_copy, 8, "wait_recv")
    total = ws_send[dp].astype(F32)
    for at in range(1, 8):
        total += ws_recv[at].astype(F32)
    weight_out[dp] = total.astype(BF)
    each(wa_copy, 8, "start")

    each(mg_copy, 16, "wait_recv")
    for p in range(16):
        mixed_out[:, p * 128 : p * 128 + 128] = mg_recv[p]

    each(fa_copy, 8, "wait_recv")
    each(wa_copy, 8, "wait_recv")
    each(mixed_copy, 16, "wait_send")
    each(mg_copy, 16, "wait_send")
    for copy in (q_copy, g_copy, w_copy, conv_copy, cg_copy, qg_copy, block_copy, wg_copy):
        each(copy, 4, "wait_send")
    for copy in (f_copy, fa_copy, ws_copy, wa_copy):
        each(copy, 8, "wait_send")


def shards(queries, key_proj, value_proj, filters, out_weight, out_grad):
    tables = make_tables()
    vm = pltpu.VMEM
    dma = pltpu.SemaphoreType.DMA
    scratch = [
        vm((128, 2048), BF), vm((128, 2048), BF), vm((128, 2048), BF), vm((16, 128, 128), F32),
        vm((512, 256), BF), vm((256, 512), BF), vm((16, 256, 256), BF), vm((16, 256, 256), BF),
        vm((16, 128, 128), BF), vm((16, 128, 128), BF),
        vm((4, 4, 128, 128), BF), vm((4, 4, 128, 128), BF),
        vm((4, 128, 2048), BF), vm((4, 128, 2048), BF),
        vm((16, 128, 128), BF), vm((4, 4, 128, 128), BF),
        vm((4, 4, 128, 128), BF),
        vm((4, 4, 128, 128), BF), vm((16, 128, 128), BF),
        vm((512, 512), BF), vm((512, 512), BF),
        vm((4, 4, 128, 128), BF), vm((4, 4, 128, 128), BF),
        vm((4, 128, 2048), BF), vm((4, 128, 2048), BF),
        vm((4, 128, 2048), BF), vm((4, 128, 2048), BF),
        vm((16, 128, 128), BF), vm((16, 128, 128), BF),
        vm((8, 2, 128, 128), BF), vm((8, 2, 128, 128), BF),
        vm((8, 16, 2048), BF), vm((8, 16, 2048), BF),
        vm((16, 8, 32, 128), BF), vm((16, 8, 32, 128), BF), vm((16, 8, 32, 256), BF),
        vm((16, 256, 128), F32), vm((16, 256, 128), F32),
        dma((10,)),
    ]
    for count in (16, 4, 4, 4, 4, 4, 4, 4, 4, 16, 8, 8, 8, 8):
        scratch += [dma((count,)), dma((count,))]
    anywhere = pl.BlockSpec(memory_space=pl.ANY)
    block, query, mixed, filt, weight = pl.pallas_call(
        kernel,
        name="hyena_block",
        out_shape=(
            jax.ShapeDtypeStruct((128, 2048), BF),
            jax.ShapeDtypeStruct((128, 2048), BF),
            jax.ShapeDtypeStruct((128, 2048), BF),
            jax.ShapeDtypeStruct((8, 2, 128, 128), BF),
            jax.ShapeDtypeStruct((8, 16, 2048), BF),
        ),
        in_specs=[anywhere] * 10,
        out_specs=[pl.BlockSpec(memory_space=pltpu.VMEM)] * 5,
        scratch_shapes=scratch,
        compiler_params=pltpu.CompilerParams(
            collective_id=0, has_side_effects=True, vmem_limit_bytes=58 << 20
        ),
    )(
        queries[0], key_proj[0], value_proj[0], filters.reshape(16, 128, 128), out_weight,
        out_grad[0], *tables,
    )
    wide = mixed.astype(F32)
    key_grad = (wide * value_proj[0].astype(F32)).astype(BF)
    value_grad = (wide * key_proj[0].astype(F32)).astype(BF)
    scale = 1.0 / math.sqrt(16384.0)
    return (
        block[None],
        query[None],
        key_grad[None],
        value_grad[None],
        filt.astype(F32).reshape(2048, 128) * scale,
        weight.astype(F32).reshape(128, 2048) * scale,
    )


def solution(mesh):
    rows = P("dp", "ctx", None)
    return jax.shard_map(
        shards,
        mesh=mesh,
        in_specs=(rows, rows, rows, P(None, "ctx"), P("ctx", None), rows),
        out_specs=(rows, rows, rows, rows, P(None, "ctx"), P("ctx", None)),
        check_vma=False,
    )
```

profile of v0, /device:TPU:2, one launch (start us, length us, event | category | flops | bytes accessed | tf_op | source)
XLA Modules:
  0.0 112.3 jit_solution(3144355117664743513)
XLA Ops:
  0.6 0.0 copy-start
  0.6 0.0 copy-start.1
  0.7 105.4 %hyena_block.1 = (bf16[128,2048]{1,0:T(8,128)(2,1)}, bf16[128,2048]{1,0:T(8,128)(2,1)}, bf16[128,2048]{1,0:T(8,128)(2,1)}, bf16[8,2,128,128]{3,2,1,0:T(8,128)(2,1)}, bf16[8,16,2048]{2,1,0:T(8,128)(2,1)}) custom-call(bf16[128,2048]{1,0:T(8,128)(2,1)} %bitcast.20, bf16[128,2048]{1,0:T(8,128)(2,1)} %bitcast.15, bf16[128,2048]{1,0:T(8,128)(2,1)} %bitcast.16, ...), custom_call_target="tpu_custom_call" | custom-call | tf_op jit(solution)/shard_map/hyena_block/pallas_call | solution.py:396
  106.1 0.0 copy-start.3
  106.1 0.0 copy-done
  106.1 0.0 copy-done.1
  106.1 0.0 copy-start.2
  106.1 2.4 %fusion.2 = (bf16[1,128,2048]{2,1,0:T(8,128)(2,1)}, bf16[1,128,2048]{2,1,0:T(8,128)(2,1)}) fusion(bf16[128,2048]{1,0:T(8,128)(2,1)} %get-tuple-element.13, bf16[1,128,2048]{2,1,0:T(8,128)(2,1)S(1)} %copy-done, bf16[1,128,2048]{2,1,0:T(8,128)(2,1)S(1)} %copy-done.1), kind=kLoop, calls=%fused_computation.6 | loop fusion | flops 1835008 | bytes 2621440 | tf_op jit(solution)/shard_map/broadcast_in_dim | solution.py:424
  108.5 0.0 copy-start.5
  108.5 0.0 copy-done.3
  108.5 0.0 copy-start.4
  108.5 1.1 convert_multiply_fusion.3
  109.6 0.0 copy-done.2
  109.6 1.1 convert_multiply_fusion.2
  110.7 0.0 copy-done.5
  110.7 0.8 copy.18
  111.5 0.0 copy-done.4
  111.5 0.8 copy.19
Async XLA Ops:
  0.6 105.4 %copy-start = (bf16[1,128,2048]{2,1,0:T(8,128)(2,1)S(1)}, bf16[1,128,2048]{2,1,0:T(8,128)(2,1)}, u32[]{:S(2)}) copy-start(bf16[1,128,2048]{2,1,0:T(8,128)(2,1)} %param.11) | copy-start | bytes 1572868
  0.6 105.4 %copy-start.1 = (bf16[1,128,2048]{2,1,0:T(8,128)(2,1)S(1)}, bf16[1,128,2048]{2,1,0:T(8,128)(2,1)}, u32[]{:S(2)}) copy-start(bf16[1,128,2048]{2,1,0:T(8,128)(2,1)} %param.12) | copy-start | bytes 1572868
  106.1 2.5 %copy-start.3 = (bf16[8,2,128,128]{3,2,1,0:T(8,128)(2,1)S(1)}, bf16[8,2,128,128]{3,2,1,0:T(8,128)(2,1)}, u32[]{:S(2)}) copy-start(bf16[8,2,128,128]{3,2,1,0:T(8,128)(2,1)} %get-tuple-element.14) | copy-start | bytes 1572868
  106.1 3.5 %copy-start.2 = (bf16[8,16,2048]{2,1,0:T(8,128)(2,1)S(1)}, bf16[8,16,2048]{2,1,0:T(8,128)(2,1)}, u32[]{:S(2)}) copy-start(bf16[8,16,2048]{2,1,0:T(8,128)(2,1)} %get-tuple-element.15) | copy-start | bytes 1572868
  108.5 2.2 %copy-start.5 = (bf16[128,2048]{1,0:T(8,128)(2,1)S(1)}, bf16[128,2048]{1,0:T(8,128)(2,1)}, u32[]{:S(2)}) copy-start(bf16[128,2048]{1,0:T(8,128)(2,1)} %get-tuple-element.11) | copy-start | bytes 1572868
  108.5 3.0 %copy-start.4 = (bf16[128,2048]{1,0:T(8,128)(2,1)S(1)}, bf16[128,2048]{1,0:T(8,128)(2,1)}, u32[]{:S(2)}) copy-start(bf16[128,2048]{1,0:T(8,128)(2,1)} %get-tuple-element.12) | copy-start | bytes 1572868
where the time goes:
time: 113 us; the launch traced here: 112 us
  Pallas kernels  105 us (93%)
  other arithmetic  4.57 us (4%)
  local copies, waits for them, and re-layouts  1.61 us (1%)
    pallas_call x1, Pallas kernels, shards(): pl.pallas_call(kernel, name='hyena_block', out_shape=(jax.ShapeDtypeStruc...  105 us
    broadcast_in_dim x1, other arithmetic, shards(): value_grad[None]  2.41 us

commit v1 on v0

--- a/solution.py
+++ b/solution.py
@@ -68,23 +68,34 @@
     q_v, k_v, v_v, h_v, p1, p1t, m_t, mt_t,
     mixed_send, mixed_recv, q_send, q_tile, g_tile, w_tile,
     conv_send, conv_tile, gg_tile, cg_send, cg_recv, gated, gated_t,
-    qg_send, qg_recv, block_send, block_recv, wg_send, wg_recv,
-    mg_send, mg_recv, f_send, f_recv, ws_send, ws_recv,
+    qg_send, qg_recv, block_send, block_core, block_red, block_far,
+    wga_send, wga_recv, wgb_send, wgb_recv, wsa_send, wsa_recv, wsb_send, wsb_recv,
+    wx_send, wx_recv, mg_send, mg_recv, f_send, f_recv, fx_send, fx_recv,
     s_buf, u_buf, u2_buf, h_spec, m_spec,
     lsem,
-    mixed_s, mixed_r, q_s, q_r, g_s, g_r, w_s, w_r, conv_s, conv_r, cg_s, cg_r, qg_s, qg_r,
-    block_s, block_r, wg_s, wg_r, mg_s, mg_r, f_s, f_r, fa_s, fa_r, ws_s, ws_r, wa_s, wa_r,
+    mixed_s, mixed_r, mg_s, mg_r, q_s, q_r, w_s, w_r, wq_s, wq_r, wf_s, wf_r, conv_s, conv_r,
+    cg_s, cg_r, qg_s, qg_r, wga_s, wga_r, wgb_s, wgb_r, wsa_s, wsa_r, wsb_s, wsb_r, wa_s, wa_r,
+    f_s, f_r, fa_s, fa_r, g_s, g_r, block_s, block_r, x_s, x_r,
 ):
     dp = lax.axis_index("dp")
     me = lax.axis_index("ctx")
     i = lax.div(me, 4)
     j = lax.rem(me, 4)
+    far = lax.div(j, 2)
+    core = lax.rem(j, 2)
+    z = lax.rem(dp, 4)
+    j_core = far * 2 + (1 - core)
+    j_far = (1 - far) * 2 + core
+    near = lax.rem(dp + 4, 8)
 
     def ctx_peer(at):
         return lax.rem(me + at, 16)
 
-    def dp_peer(at):
-        return lax.rem(dp + at, 8)
+    def z_peer(at):
+        return lax.rem(z + at, 4)
+
+    def to_z(at):
+        return dp - z + z_peer(at)
 
     def i_peer(at):
         return lax.rem(i + at, 4)
@@ -110,11 +121,41 @@
         p = j_peer(at)
         return remote(q_send.at[p], q_tile.at[:, j], q_s.at[at], q_r.at[at], dp, i * 4 + p)
 
-    def g_copy(at):
-        return remote(g_in, g_tile.at[j], g_s.at[at], g_r.at[at], dp, i * 4 + j_peer(at))
+    def g_core(at):
+        rows = pl.ds(at * 64, 64)
+        return remote(
+            g_in.at[rows], g_tile.at[j, rows], g_s.at[at], g_r.at[at], dp, i * 4 + j_core
+        )
+
+    def g_far(at):
+        rows = pl.ds(at * 64, 64)
+        return remote(
+            g_in.at[rows], g_tile.at[j, rows], g_s.at[2 + at], g_r.at[2 + at], dp, i * 4 + j_far
+        )
+
+    def g_pass(at):
+        rows = pl.ds(at * 64, 64)
+        ref = g_tile.at[j_far, rows]
+        return remote(ref, ref, g_s.at[4 + at], g_r.at[4 + at], dp, i * 4 + j_core)
 
     def w_copy(at):
-        return remote(w_in, w_tile.at[i], w_s.at[at], w_r.at[at], dp, i_peer(at) * 4 + j)
+        rows = pl.ds(0, 64)
+        return remote(
+            w_in.at[rows], w_tile.at[i, rows], w_s.at[at], w_r.at[at], dp, i_peer(at) * 4 + j
+        )
+
+    def w_rows():
+        return pl.ds(pl.multiple_of(64 + z * 16, 16), 16)
+
+    def wq_copy(at):
+        return remote(
+            w_in.at[w_rows()], w_tile.at[i, w_rows()], wq_s.at[at], wq_r.at[at],
+            dp, i_peer(at) * 4 + j,
+        )
+
+    def wf_copy(at):
+        ref = w_tile.at[i_peer(1 + lax.rem(at, 3)), w_rows()]
+        return remote(ref, ref, wf_s.at[at], wf_r.at[at], to_z(1 + lax.div(at, 3)), me)
 
     def conv_copy(at):
         p = i_peer(at)
@@ -133,31 +174,48 @@
         p = j_peer(at)
         return remote(qg_send.at[p], qg_recv.at[j], qg_s.at[at], qg_r.at[at], dp, i * 4 + p)
 
-    def block_copy(at):
-        p = j_peer(at)
-        return remote(
-            block_send.at[p], block_recv.at[at], block_s.at[at], block_r.at[at], dp, i * 4 + p
-        )
-
-    def wg_copy(at):
+    def block_near(at):
+        return remote(
+            block_send.at[at * 2 + 1 - core], block_core.at[at], block_s.at[at], block_r.at[at],
+            dp, i * 4 + j_core,
+        )
+
+    def block_cross(at):
+        return remote(block_red, block_far, block_s.at[2], block_r.at[2], dp, i * 4 + j_far)
+
+    def wga_copy(at):
         p = i_peer(at)
-        return remote(wg_send.at[p], wg_recv.at[at], wg_s.at[at], wg_r.at[at], dp, p * 4 + j)
+        return remote(wga_send.at[p], wga_recv.at[at], wga_s.at[at], wga_r.at[at], dp, p * 4 + j)
+
+    def wgb_copy(at):
+        rows = pl.ds(pl.multiple_of(z_peer(at) * 32, 32), 32)
+        return remote(
+            wgb_send.at[:, rows], wgb_recv.at[at], wgb_s.at[at], wgb_r.at[at], to_z(at), me
+        )
+
+    def wsa_copy(at):
+        return remote(
+            wsa_send.at[z_peer(at)], wsa_recv.at[at], wsa_s.at[at], wsa_r.at[at], to_z(at), me
+        )
+
+    def wsb_copy(at):
+        p = i_peer(at)
+        return remote(wsb_send.at[p], wsb_recv.at[at], wsb_s.at[at], wsb_r.at[at], dp, p * 4 + j)
+
+    def wx_copy(at):
+        return remote(wx_send, wx_recv, x_s.at[0], x_r.at[0], near, me)
+
+    def wa_copy(at):
+        return remote(weight_out.at[z], weight_out.at[z], wa_s.at[at], wa_r.at[at], to_z(at), me)
 
     def f_copy(at):
-        p = dp_peer(at)
-        return remote(f_send.at[p], f_recv.at[at], f_s.at[at], f_r.at[at], p, me)
+        return remote(f_send.at[z_peer(at)], f_recv.at[at], f_s.at[at], f_r.at[at], to_z(at), me)
+
+    def fx_copy(at):
+        return remote(fx_send, fx_recv, x_s.at[1], x_r.at[1], near, me)
 
     def fa_copy(at):
-        p = dp_peer(at)
-        return remote(filter_out.at[dp], filter_out.at[dp], fa_s.at[at], fa_r.at[at], p, me)
-
-    def ws_copy(at):
-        p = dp_peer(at)
-        return remote(ws_send.at[p], ws_recv.at[at], ws_s.at[at], ws_r.at[at], p, me)
-
-    def wa_copy(at):
-        p = dp_peer(at)
-        return remote(weight_out.at[dp], weight_out.at[dp], wa_s.at[at], wa_r.at[at], p, me)
+        return remote(filter_out.at[z], filter_out.at[z], fa_s.at[at], fa_r.at[at], to_z(at), me)
 
     def each(copy, n, what):
         loop(n - 1, lambda at: getattr(copy(at + 1), what)())
@@ -181,11 +239,12 @@
             barrier, inc=1, device_id=(dp, ctx_peer(at + 1)), device_id_type=MESH
         )
 
-    def greet_dp(at):
-        pl.semaphore_signal(barrier, inc=1, device_id=(dp_peer(at + 1), me), device_id_type=MESH)
+    def greet_z(at):
+        pl.semaphore_signal(barrier, inc=1, device_id=(to_z(at + 1), me), device_id_type=MESH)
 
     loop(15, greet_ctx)
-    loop(7, greet_dp)
+    loop(3, greet_z)
+    pl.semaphore_signal(barrier, inc=1, device_id=(near, me), device_id_type=MESH)
 
     local[0].wait()
     local[1].wait()
@@ -196,11 +255,14 @@
     for p in range(16):
         q_send[p % 4, p // 4] = q_v[:, p * 128 : p * 128 + 128]
 
-    pl.semaphore_wait(barrier, 22)
+    pl.semaphore_wait(barrier, 19)
     each(mixed_copy, 16, "start")
+    each(wq_copy, 4, "start")
+    for at in range(2):
+        g_far(at).start()
+        g_core(at).start()
     each(q_copy, 4, "start")
     each(w_copy, 4, "start")
-    each(g_copy, 4, "start")
     mixed_recv[me] = mixed_send[me]
     q_tile[:, j] = q_send[j]
 
@@ -222,6 +284,9 @@
         h_spec[k0] = inner(k0)
 
     loop(16, filter_step, 2)
+
+    each(wq_copy, 4, "wait_recv")
+    loop(9, lambda at: wf_copy(at).start())
 
     each(mixed_copy, 16, "wait_recv")
     outer_step(mixed_recv)
@@ -242,11 +307,18 @@
     each(conv_copy, 4, "start")
     conv_tile[i] = conv_send[pl.ds(i * 4, 4)]
 
+    for at in range(2):
+        g_far(at).wait_recv()
+        g_pass(at).start()
+
     local[8].wait()
     local[9].wait()
     each(q_copy, 4, "wait_recv")
     each(w_copy, 4, "wait_recv")
-    each(g_copy, 4, "wait_recv")
+    loop(9, lambda at: wf_copy(at).wait_recv())
+    for at in range(2):
+        g_core(at).wait_recv()
+        g_pass(at).wait_recv()
     for half in range(2):
         wide = lax.dot_general(
             g_tile[...].reshape(512, 2048),
@@ -274,21 +346,37 @@
     each(qg_copy, 4, "start")
     qg_recv[j] = qg_send[j]
 
-    def wg_step(n):
-        lanes = pl.ds(pl.multiple_of(n * 256, 256), 256)
-        y = dot(gated_t[...], g_tile[:, :, lanes].reshape(512, 256))
-        wg_send[:, :, lanes] = y.astype(BF).reshape(4, 128, 256)
-
-    loop(8, wg_step)
-    each(wg_copy, 4, "start")
-
     def block_step(n):
         lanes = pl.ds(pl.multiple_of(n * 256, 256), 256)
         y = dot(gated[...], w_tile[:, :, lanes].reshape(512, 256))
         block_send[:, :, lanes] = y.astype(BF).reshape(4, 128, 256)
 
     loop(8, block_step)
-    each(block_copy, 4, "start")
+    for at in range(2):
+        block_near(at).start()
+
+    def wg_step(out, n, first):
+        lanes = pl.ds(pl.multiple_of(n * 256, 256), 256)
+        cols = pl.ds(pl.multiple_of(first + n * 256, 256), 256)
+        y = dot(gated_t[...], g_tile[:, :, cols].reshape(512, 256))
+        out[:, :, lanes] = y.astype(BF).reshape(4, 128, 256)
+
+    loop(4, lambda n: wg_step(wga_send, n, 0))
+    each(wga_copy, 4, "start")
+    loop(4, lambda n: wg_step(wgb_send, n, 1024))
+    each(wgb_copy, 4, "start")
+
+    for at in range(2):
+        block_near(at).wait_recv()
+
+    def bred_step(r):
+        block_red[rows16(r), :] = (
+            block_send[j_far, rows16(r), :].astype(F32)
+            + block_core[1 - far, rows16(r), :].astype(F32)
+        ).astype(BF)
+
+    loop(8, bred_step)
+    block_cross(0).start()
 
     each(cg_copy, 4, "wait_recv")
     outer_step(cg_recv)
@@ -306,64 +394,95 @@
         y = dot(p1t[...], u2_buf[:, g].reshape(512, 256)) * (1.0 / 2048.0)
         y = y.reshape(16, 16, 256).astype(BF)
         mg_send[:, rows16(g), :] = y[:, :, :128]
-        f_send[:, :, rows16(g), :] = y[:, :, 128:].reshape(8, 2, 16, 128)
+        f_send[:, :, rows16(g), :] = y[:, :, 128:].reshape(4, 4, 16, 128)
 
     loop(8, back_last, 2)
     each(mg_copy, 16, "start")
-    each(f_copy, 8, "start")
+    each(f_copy, 4, "start")
     mg_recv[me] = mg_send[me]
 
     each(qg_copy, 4, "wait_recv")
     for p in range(16):
         query_out[:, p * 128 : p * 128 + 128] = qg_recv[p % 4, p // 4]
 
-    each(wg_copy, 4, "wait_recv")
-
-    def wsum_step(r):
-        total = wg_send[i, rows16(r), :].astype(F32)
+    each(wga_copy, 4, "wait_recv")
+
+    def suma_step(r):
+        total = wga_send[i, rows16(r), :].astype(F32)
         for at in range(1, 4):
-            total += wg_recv[at, rows16(r), :].astype(F32)
-        ws_send[r] = total.astype(BF)
-
-    loop(8, wsum_step)
-    each(ws_copy, 8, "start")
-
-    each(f_copy, 8, "wait_recv")
-    total = f_send[dp].astype(F32)
-    for at in range(1, 8):
+            total += wga_recv[at, rows16(r), :].astype(F32)
+        wsa_send[lax.div(r, 2), rows16(lax.rem(r, 2)), :] = total.astype(BF)
+
+    loop(8, suma_step)
+    each(wsa_copy, 4, "start")
+    each(wgb_copy, 4, "wait_recv")
+
+    def sumb_step(r):
+        total = wgb_send[r, pl.ds(pl.multiple_of(z * 32, 32), 32), :].astype(F32)
+        for at in range(1, 4):
+            total += wgb_recv[at, r].astype(F32)
+        wsb_send[r] = total.astype(BF)
+
+    loop(4, sumb_step)
+    each(wsb_copy, 4, "start")
+
+    each(f_copy, 4, "wait_recv")
+    total = f_send[z].astype(F32)
+    for at in range(1, 4):
         total += f_recv[at].astype(F32)
-    filter_out[dp] = total.astype(BF)
-    each(fa_copy, 8, "start")
-
-    each(block_copy, 4, "wait_recv")
+    fx_send[...] = total.astype(BF)
+    fx_copy(0).start()
+
+    each(wsa_copy, 4, "wait_recv")
+    total = wsa_send[z].astype(F32)
+    for at in range(1, 4):
+        total += wsa_recv[at].astype(F32)
+    wx_send[:, :1024] = total.astype(BF)
+    each(wsb_copy, 4, "wait_recv")
+    total = wsb_send[i].astype(F32)
+    for at in range(1, 4):
+        total += wsb_recv[at].astype(F32)
+    wx_send[:, 1024:] = total.astype(BF)
+    wx_copy(0).start()
+
+    fx_copy(0).wait_recv()
+    filter_out[z] = (fx_send[...].astype(F32) + fx_recv[...].astype(F32)).astype(BF)
+    each(fa_copy, 4, "start")
+
+    block_cross(0).wait_recv()
 
     def bsum_step(r):
-        total = block_send[j, rows16(r), :].astype(F32)
-        for at in range(1, 4):
-            total += block_recv[at, rows16(r), :].astype(F32)
-        block_out[rows16(r), :] = total.astype(BF)
+        block_out[rows16(r), :] = (
+            block_send[j, rows16(r), :].astype(F32)
+            + block_core[far, rows16(r), :].astype(F32)
+            + block_far[rows16(r), :].astype(F32)
+        ).astype(BF)
 
     loop(8, bsum_step)
 
-    each(ws_copy, 8, "wait_recv")
-    total = ws_send[dp].astype(F32)
-    for at in range(1, 8):
-        total += ws_recv[at].astype(F32)
-    weight_out[dp] = total.astype(BF)
-    each(wa_copy, 8, "start")
+    wx_copy(0).wait_recv()
+    weight_out[z] = (wx_send[...].astype(F32) + wx_recv[...].astype(F32)).astype(BF)
+    each(wa_copy, 4, "start")
 
     each(mg_copy, 16, "wait_recv")
     for p in range(16):
         mixed_out[:, p * 128 : p * 128 + 128] = mg_recv[p]
 
-    each(fa_copy, 8, "wait_recv")
-    each(wa_copy, 8, "wait_recv")
+    each(fa_copy, 4, "wait_recv")
+    each(wa_copy, 4, "wait_recv")
     each(mixed_copy, 16, "wait_send")
     each(mg_copy, 16, "wait_send")
-    for copy in (q_copy, g_copy, w_copy, conv_copy, cg_copy, qg_copy, block_copy, wg_copy):
+    for copy in (
+        q_copy, w_copy, wq_copy, conv_copy, cg_copy, qg_copy, wga_copy, wgb_copy, wsa_copy,
+        wsb_copy, wa_copy, f_copy, fa_copy,
+    ):
         each(copy, 4, "wait_send")
-    for copy in (f_copy, fa_copy, ws_copy, wa_copy):
-        each(copy, 8, "wait_send")
+    loop(9, lambda at: wf_copy(at).wait_send())
+    for at in range(2):
+        for copy in (g_core, g_far, g_pass, block_near):
+            copy(at).wait_send()
+    for copy in (block_cross, wx_copy, fx_copy):
+        copy(0).wait_send()
 
 
 def shards(queries, key_proj, value_proj, filters, out_weight, out_grad):
@@ -381,16 +500,21 @@
         vm((4, 4, 128, 128), BF), vm((16, 128, 128), BF),
         vm((512, 512), BF), vm((512, 512), BF),
         vm((4, 4, 128, 128), BF), vm((4, 4, 128, 128), BF),
-        vm((4, 128, 2048), BF), vm((4, 128, 2048), BF),
-        vm((4, 128, 2048), BF), vm((4, 128, 2048), BF),
+        vm((4, 128, 2048), BF), vm((2, 128, 2048), BF),
+        vm((128, 2048), BF), vm((128, 2048), BF),
+        vm((4, 128, 1024), BF), vm((4, 128, 1024), BF),
+        vm((4, 128, 1024), BF), vm((4, 4, 32, 1024), BF),
+        vm((4, 32, 1024), BF), vm((4, 32, 1024), BF),
+        vm((4, 32, 1024), BF), vm((4, 32, 1024), BF),
+        vm((32, 2048), BF), vm((32, 2048), BF),
         vm((16, 128, 128), BF), vm((16, 128, 128), BF),
-        vm((8, 2, 128, 128), BF), vm((8, 2, 128, 128), BF),
-        vm((8, 16, 2048), BF), vm((8, 16, 2048), BF),
+        vm((4, 4, 128, 128), BF), vm((4, 4, 128, 128), BF),
+        vm((4, 128, 128), BF), vm((4, 128, 128), BF),
         vm((16, 8, 32, 128), BF), vm((16, 8, 32, 128), BF), vm((16, 8, 32, 256), BF),
         vm((16, 256, 128), F32), vm((16, 256, 128), F32),
         dma((10,)),
     ]
-    for count in (16, 4, 4, 4, 4, 4, 4, 4, 4, 16, 8, 8, 8, 8):
+    for count in (16, 16, 4, 4, 4, 9, 4, 4, 4, 4, 4, 4, 4, 4, 4, 4, 6, 3, 2):
         scratch += [dma((count,)), dma((count,))]
     anywhere = pl.BlockSpec(memory_space=pl.ANY)
     block, query, mixed, filt, weight = pl.pallas_call(
@@ -400,8 +524,8 @@
             jax.ShapeDtypeStruct((128, 2048), BF),
             jax.ShapeDtypeStruct((128, 2048), BF),
             jax.ShapeDtypeStruct((128, 2048), BF),
-            jax.ShapeDtypeStruct((8, 2, 128, 128), BF),
-            jax.ShapeDtypeStruct((8, 16, 2048), BF),
+            jax.ShapeDtypeStruct((4, 4, 128, 128), BF),
+            jax.ShapeDtypeStruct((4, 32, 2048), BF),
         ),
         in_specs=[anywhere] * 10,
         out_specs=[pl.BlockSpec(memory_space=pltpu.VMEM)] * 5,

time: 113 us -> 88.8 us (0.79)
  Pallas kernels: 105 us -> 81.7 us
    pallas_call x1, Pallas kernels: 105 us -> 81.7 us  [shards(): pl.pallas_call(kernel, name='hyena_block', out_shape=(jax.ShapeDtypeStruc...]
where the time goes in v1:
time: 88.8 us; the launch traced here: 88.6 us
  Pallas kernels  81.7 us (92%)
  other arithmetic  4.57 us (5%)
  local copies, waits for them, and re-layouts  1.61 us (2%)
    pallas_call x1, Pallas kernels, shards(): pl.pallas_call(kernel, name='hyena_block', out_shape=(jax.ShapeDtypeStruc...  81.7 us
    broadcast_in_dim x1, other arithmetic, shards(): value_grad[None]  2.41 us

profile of v1, /device:TPU:2, one launch (start us, length us, event | category | flops | bytes accessed | tf_op | source)
XLA Modules:
  0.0 88.6 jit_solution(14464382100687529980)
XLA Ops:
  0.6 0.0 copy-start
  0.6 0.0 copy-start.1
  0.7 81.7 %hyena_block.1 = (bf16[128,2048]{1,0:T(8,128)(2,1)}, bf16[128,2048]{1,0:T(8,128)(2,1)}, bf16[128,2048]{1,0:T(8,128)(2,1)}, bf16[4,4,128,128]{3,2,1,0:T(8,128)(2,1)}, bf16[4,32,2048]{2,1,0:T(8,128)(2,1)}) custom-call(bf16[128,2048]{1,0:T(8,128)(2,1)} %bitcast.20, bf16[128,2048]{1,0:T(8,128)(2,1)} %bitcast.15, bf16[128,2048]{1,0:T(8,128)(2,1)} %bitcast.16, ...), custom_call_target="tpu_custom_call" | custom-call | tf_op jit(solution)/shard_map/hyena_block/pallas_call | solution.py:520
  82.4 0.0 copy-start.3
  82.4 0.0 copy-done
  82.4 0.0 copy-done.1
  82.4 0.0 copy-start.2
  82.4 2.4 %fusion.2 = (bf16[1,128,2048]{2,1,0:T(8,128)(2,1)}, bf16[1,128,2048]{2,1,0:T(8,128)(2,1)}) fusion(bf16[128,2048]{1,0:T(8,128)(2,1)} %get-tuple-element.13, bf16[1,128,2048]{2,1,0:T(8,128)(2,1)S(1)} %copy-done, bf16[1,128,2048]{2,1,0:T(8,128)(2,1)S(1)} %copy-done.1), kind=kLoop, calls=%fused_computation.6 | loop fusion | flops 1835008 | bytes 2621440 | tf_op jit(solution)/shard_map/broadcast_in_dim | solution.py:548
  84.8 0.0 copy-start.5
  84.8 0.0 copy-done.3
  84.8 0.0 copy-start.4
  84.8 1.1 %convert_multiply_fusion.3 = f32[4,4,128,128]{3,2,1,0:T(8,128)} fusion(bf16[4,4,128,128]{3,2,1,0:T(8,128)(2,1)S(1)} %copy-done.3), kind=kLoop, calls=%fused_computation.5 | loop fusion | flops 524288 | bytes 1572864 | tf_op jit(solution)/shard_map/mul | solution.py:549
  85.9 0.0 copy-done.2
  85.9 1.1 %convert_multiply_fusion.2 = f32[4,32,2048]{2,1,0:T(8,128)} fusion(bf16[4,32,2048]{2,1,0:T(8,128)(2,1)S(1)} %copy-done.2), kind=kLoop, calls=%fused_computation.4 | loop fusion | flops 524288 | bytes 1572864 | tf_op jit(solution)/shard_map/mul | solution.py:550
  87.0 0.0 copy-done.5
  87.0 0.8 copy.18
  87.8 0.0 copy-done.4
  87.8 0.8 copy.19
Async XLA Ops:
  0.6 81.8 %copy-start = (bf16[1,128,2048]{2,1,0:T(8,128)(2,1)S(1)}, bf16[1,128,2048]{2,1,0:T(8,128)(2,1)}, u32[]{:S(2)}) copy-start(bf16[1,128,2048]{2,1,0:T(8,128)(2,1)} %param.11) | copy-start | bytes 1572868
  0.6 81.8 %copy-start.1 = (bf16[1,128,2048]{2,1,0:T(8,128)(2,1)S(1)}, bf16[1,128,2048]{2,1,0:T(8,128)(2,1)}, u32[]{:S(2)}) copy-start(bf16[1,128,2048]{2,1,0:T(8,128)(2,1)} %param.12) | copy-start | bytes 1572868
  82.4 2.5 %copy-start.3 = (bf16[4,4,128,128]{3,2,1,0:T(8,128)(2,1)S(1)}, bf16[4,4,128,128]{3,2,1,0:T(8,128)(2,1)}, u32[]{:S(2)}) copy-start(bf16[4,4,128,128]{3,2,1,0:T(8,128)(2,1)} %get-tuple-element.14) | copy-start | bytes 1572868
  82.4 3.5 %copy-start.2 = (bf16[4,32,2048]{2,1,0:T(8,128)(2,1)S(1)}, bf16[4,32,2048]{2,1,0:T(8,128)(2,1)}, u32[]{:S(2)}) copy-start(bf16[4,32,2048]{2,1,0:T(8,128)(2,1)} %get-tuple-element.15) | copy-start | bytes 1572868
  84.8 2.2 %copy-start.5 = (bf16[128,2048]{1,0:T(8,128)(2,1)S(1)}, bf16[128,2048]{1,0:T(8,128)(2,1)}, u32[]{:S(2)}) copy-start(bf16[128,2048]{1,0:T(8,128)(2,1)} %get-tuple-element.11) | copy-start | bytes 1572868
  84.8 3.0 %copy-start.4 = (bf16[128,2048]{1,0:T(8,128)(2,1)S(1)}, bf16[128,2048]{1,0:T(8,128)(2,1)}, u32[]{:S(2)}) copy-start(bf16[128,2048]{1,0:T(8,128)(2,1)} %get-tuple-element.12) | copy-start | bytes 1572868

commit v2 on v1

--- a/solution.py
+++ b/solution.py
@@ -64,7 +64,7 @@
 
 def kernel(
     q_in, k_in, v_in, h_in, w_in, g_in, p1_in, p1t_in, m_in, mt_in,
-    block_out, query_out, mixed_out, filter_out, weight_out,
+    block_out, query_out, key_out, value_out, filter_out, weight_out,
     q_v, k_v, v_v, h_v, p1, p1t, m_t, mt_t,
     mixed_send, mixed_recv, q_send, q_tile, g_tile, w_tile,
     conv_send, conv_tile, gg_tile, cg_send, cg_recv, gated, gated_t,
@@ -72,7 +72,7 @@
     wga_send, wga_recv, wgb_send, wgb_recv, wsa_send, wsa_recv, wsb_send, wsb_recv,
     wx_send, wx_recv, mg_send, mg_recv, f_send, f_recv, fx_send, fx_recv,
     s_buf, u_buf, u2_buf, h_spec, m_spec,
-    lsem,
+    f_total, w_total, block_v, key_v, value_v, lsem, osem,
     mixed_s, mixed_r, mg_s, mg_r, q_s, q_r, w_s, w_r, wq_s, wq_r, wf_s, wf_r, conv_s, conv_r,
     cg_s, cg_r, qg_s, qg_r, wga_s, wga_r, wgb_s, wgb_r, wsa_s, wsa_r, wsb_s, wsb_r, wa_s, wa_r,
     f_s, f_r, fa_s, fa_r, g_s, g_r, block_s, block_r, x_s, x_r,
@@ -164,11 +164,18 @@
             dp, p * 4 + j,
         )
 
-    def cg_copy(at):
+    def cg_half(at, side, first):
         p = i_peer(at)
         return remote(
-            cg_send.at[p], cg_recv.at[pl.ds(i * 4, 4)], cg_s.at[at], cg_r.at[at], dp, p * 4 + j
-        )
+            cg_send.at[p, pl.ds(side * 2, 2)], cg_recv.at[pl.ds(i * 4 + side * 2, 2)],
+            cg_s.at[first + at], cg_r.at[first + at], dp, p * 4 + j,
+        )
+
+    def cg_mine(at):
+        return cg_half(at, far, 0)
+
+    def cg_other(at):
+        return cg_half(at, 1 - far, 4)
 
     def qg_copy(at):
         p = j_peer(at)
@@ -206,7 +213,7 @@
         return remote(wx_send, wx_recv, x_s.at[0], x_r.at[0], near, me)
 
     def wa_copy(at):
-        return remote(weight_out.at[z], weight_out.at[z], wa_s.at[at], wa_r.at[at], to_z(at), me)
+        return remote(w_total.at[z], w_total.at[z], wa_s.at[at], wa_r.at[at], to_z(at), me)
 
     def f_copy(at):
         return remote(f_send.at[z_peer(at)], f_recv.at[at], f_s.at[at], f_r.at[at], to_z(at), me)
@@ -215,7 +222,10 @@
         return remote(fx_send, fx_recv, x_s.at[1], x_r.at[1], near, me)
 
     def fa_copy(at):
-        return remote(filter_out.at[z], filter_out.at[z], fa_s.at[at], fa_r.at[at], to_z(at), me)
+        return remote(f_total.at[z], f_total.at[z], fa_s.at[at], fa_r.at[at], to_z(at), me)
+
+    def leave(at, src, dst):
+        return pltpu.make_async_copy(src, dst, osem.at[at])
 
     def each(copy, n, what):
         loop(n - 1, lambda at: getattr(copy(at + 1), what)())
@@ -229,8 +239,8 @@
             ]
         )
     ]
-    for copy in local:
-        copy.start()
+    local[0].start()
+    local[1].start()
 
     barrier = pltpu.get_barrier_semaphore()
 
@@ -248,6 +258,8 @@
 
     local[0].wait()
     local[1].wait()
+    for at in range(2, 10):
+        local[at].start()
     for p in range(16):
         lanes = slice(p * 128, p * 128 + 128)
         mixed_send[p] = (k_v[:, lanes].astype(F32) * v_v[:, lanes].astype(F32)).astype(BF)
@@ -258,11 +270,6 @@
     pl.semaphore_wait(barrier, 19)
     each(mixed_copy, 16, "start")
     each(wq_copy, 4, "start")
-    for at in range(2):
-        g_far(at).start()
-        g_core(at).start()
-    each(q_copy, 4, "start")
-    each(w_copy, 4, "start")
     mixed_recv[me] = mixed_send[me]
     q_tile[:, j] = q_send[j]
 
@@ -285,6 +292,11 @@
 
     loop(16, filter_step, 2)
 
+    for at in range(2):
+        g_far(at).start()
+        g_core(at).start()
+    each(w_copy, 4, "start")
+    each(q_copy, 4, "start")
     each(wq_copy, 4, "wait_recv")
     loop(9, lambda at: wf_copy(at).start())
 
@@ -313,25 +325,35 @@
 
     local[8].wait()
     local[9].wait()
-    each(q_copy, 4, "wait_recv")
+
+    def grad_rows(side):
+        rows = pl.ds(side * 2, 2)
+        for half in range(2):
+            wide = lax.dot_general(
+                g_tile[rows].reshape(256, 2048),
+                w_tile[2 * half : 2 * half + 2].reshape(256, 2048),
+                (((1,), (1,)), ((), ())),
+                preferred_element_type=F32,
+            ).astype(BF)
+            for at in range(2):
+                part = 2 * half + at
+                gg = wide[:, at * 128 : at * 128 + 128].reshape(2, 128, 128)
+                gg_tile[part, rows] = gg
+                cg_send[part, rows] = (
+                    gg.astype(F32) * q_tile[part, rows].astype(F32)
+                ).astype(BF)
+
     each(w_copy, 4, "wait_recv")
     loop(9, lambda at: wf_copy(at).wait_recv())
     for at in range(2):
         g_core(at).wait_recv()
+    each(q_copy, 4, "wait_recv")
+    grad_rows(far)
+    each(cg_mine, 4, "start")
+    for at in range(2):
         g_pass(at).wait_recv()
-    for half in range(2):
-        wide = lax.dot_general(
-            g_tile[...].reshape(512, 2048),
-            w_tile[2 * half : 2 * half + 2].reshape(256, 2048),
-            (((1,), (1,)), ((), ())),
-            preferred_element_type=F32,
-        ).astype(BF)
-        for at in range(2):
-            part = 2 * half + at
-            gg = wide[:, at * 128 : at * 128 + 128].reshape(4, 128, 128)
-            gg_tile[part] = gg
-            cg_send[part] = (gg.astype(F32) * q_tile[part].astype(F32)).astype(BF)
-    each(cg_copy, 4, "start")
+    grad_rows(1 - far)
+    each(cg_other, 4, "start")
     cg_recv[pl.ds(i * 4, 4)] = cg_send[i]
 
     each(conv_copy, 4, "wait_recv")
@@ -352,8 +374,8 @@
         block_send[:, :, lanes] = y.astype(BF).reshape(4, 128, 256)
 
     loop(8, block_step)
-    for at in range(2):
-        block_near(at).start()
+    block_near(1 - far).start()
+    block_near(far).start()
 
     def wg_step(out, n, first):
         lanes = pl.ds(pl.multiple_of(n * 256, 256), 256)
@@ -366,8 +388,7 @@
     loop(4, lambda n: wg_step(wgb_send, n, 1024))
     each(wgb_copy, 4, "start")
 
-    for at in range(2):
-        block_near(at).wait_recv()
+    block_near(1 - far).wait_recv()
 
     def bred_step(r):
         block_red[rows16(r), :] = (
@@ -378,7 +399,8 @@
     loop(8, bred_step)
     block_cross(0).start()
 
-    each(cg_copy, 4, "wait_recv")
+    each(cg_mine, 4, "wait_recv")
+    each(cg_other, 4, "wait_recv")
     outer_step(cg_recv)
 
     def back_step(k0):
@@ -397,13 +419,14 @@
         f_send[:, :, rows16(g), :] = y[:, :, 128:].reshape(4, 4, 16, 128)
 
     loop(8, back_last, 2)
+    each(f_copy, 4, "start")
     each(mg_copy, 16, "start")
-    each(f_copy, 4, "start")
     mg_recv[me] = mg_send[me]
 
     each(qg_copy, 4, "wait_recv")
     for p in range(16):
-        query_out[:, p * 128 : p * 128 + 128] = qg_recv[p % 4, p // 4]
+        q_v[:, p * 128 : p * 128 + 128] = qg_recv[p % 4, p // 4]
+    leave(0, q_v, query_out).start()
 
     each(wga_copy, 4, "wait_recv")
 
@@ -446,34 +469,43 @@
     wx_copy(0).start()
 
     fx_copy(0).wait_recv()
-    filter_out[z] = (fx_send[...].astype(F32) + fx_recv[...].astype(F32)).astype(BF)
+    f_total[z] = (fx_send[...].astype(F32) + fx_recv[...].astype(F32)).astype(BF)
     each(fa_copy, 4, "start")
 
+    block_near(far).wait_recv()
     block_cross(0).wait_recv()
 
     def bsum_step(r):
-        block_out[rows16(r), :] = (
+        block_v[rows16(r), :] = (
             block_send[j, rows16(r), :].astype(F32)
             + block_core[far, rows16(r), :].astype(F32)
             + block_far[rows16(r), :].astype(F32)
         ).astype(BF)
 
     loop(8, bsum_step)
+    leave(1, block_v, block_out).start()
 
     wx_copy(0).wait_recv()
-    weight_out[z] = (wx_send[...].astype(F32) + wx_recv[...].astype(F32)).astype(BF)
+    w_total[z] = (wx_send[...].astype(F32) + wx_recv[...].astype(F32)).astype(BF)
     each(wa_copy, 4, "start")
 
     each(mg_copy, 16, "wait_recv")
     for p in range(16):
-        mixed_out[:, p * 128 : p * 128 + 128] = mg_recv[p]
+        lanes = slice(p * 128, p * 128 + 128)
+        mg = mg_recv[p].astype(F32)
+        key_v[:, lanes] = (mg * v_v[:, lanes].astype(F32)).astype(BF)
+        value_v[:, lanes] = (mg * k_v[:, lanes].astype(F32)).astype(BF)
+    leave(2, key_v, key_out).start()
+    leave(5, value_v, value_out).start()
 
     each(fa_copy, 4, "wait_recv")
+    leave(3, f_total, filter_out).start()
     each(wa_copy, 4, "wait_recv")
+    leave(4, w_total, weight_out).start()
     each(mixed_copy, 16, "wait_send")
     each(mg_copy, 16, "wait_send")
     for copy in (
-        q_copy, w_copy, wq_copy, conv_copy, cg_copy, qg_copy, wga_copy, wgb_copy, wsa_copy,
+        q_copy, w_copy, wq_copy, conv_copy, cg_mine, cg_other, qg_copy, wga_copy, wgb_copy, wsa_copy,
         wsb_copy, wa_copy, f_copy, fa_copy,
     ):
         each(copy, 4, "wait_send")
@@ -483,6 +515,45 @@
             copy(at).wait_send()
     for copy in (block_cross, wx_copy, fx_copy):
         copy(0).wait_send()
+    for at, (src, dst) in enumerate(
+        [(q_v, query_out), (block_v, block_out), (key_v, key_out), (f_total, filter_out),
+         (w_total, weight_out), (value_v, value_out)]
+    ):
+        leave(at, src, dst).wait()
+
+
+def finish(
+    block_in, query_in, key_in, value_in, filter_in, weight_in,
+    block_out, query_out, key_out, value_out, filter_out, weight_out,
+    f_v, w_v, f_wide, w_wide, rows, sem,
+):
+    scale = 1.0 / math.sqrt(16384.0)
+
+    def move(at, src, dst):
+        copy = pltpu.make_async_copy(src, dst, sem.at[at])
+        copy.start()
+        return copy
+
+    loads = [
+        move(at, src, dst)
+        for at, (src, dst) in enumerate(
+            [
+                (filter_in, f_v), (weight_in, w_v), (block_in, rows.at[0]),
+                (query_in, rows.at[1]), (key_in, rows.at[2]), (value_in, rows.at[3]),
+            ]
+        )
+    ]
+    loads[0].wait()
+    f_wide[...] = f_v[...].astype(F32) * scale
+    moves = [move(6, f_wide, filter_out)]
+    loads[1].wait()
+    w_wide[...] = w_v[...].astype(F32) * scale
+    moves.append(move(7, w_wide, weight_out))
+    for at, out in enumerate((block_out, query_out, key_out, value_out)):
+        loads[2 + at].wait()
+        moves.append(move(8 + at, rows.at[at], out))
+    for copy in moves:
+        copy.wait()
 
 
 def shards(queries, key_proj, value_proj, filters, out_weight, out_grad):
@@ -512,15 +583,18 @@
         vm((4, 128, 128), BF), vm((4, 128, 128), BF),
         vm((16, 8, 32, 128), BF), vm((16, 8, 32, 128), BF), vm((16, 8, 32, 256), BF),
         vm((16, 256, 128), F32), vm((16, 256, 128), F32),
-        dma((10,)),
+        vm((4, 4, 128, 128), BF), vm((4, 32, 2048), BF),
+        vm((128, 2048), BF), vm((128, 2048), BF), vm((128, 2048), BF),
+        dma((10,)), dma((6,)),
     ]
-    for count in (16, 16, 4, 4, 4, 9, 4, 4, 4, 4, 4, 4, 4, 4, 4, 4, 6, 3, 2):
+    for count in (16, 16, 4, 4, 4, 9, 4, 8, 4, 4, 4, 4, 4, 4, 4, 4, 6, 3, 2):
         scratch += [dma((count,)), dma((count,))]
     anywhere = pl.BlockSpec(memory_space=pl.ANY)
-    block, query, mixed, filt, weight = pl.pallas_call(
+    block, query, key, value, filt, weight = pl.pallas_call(
         kernel,
         name="hyena_block",
         out_shape=(
+            jax.ShapeDtypeStruct((128, 2048), BF),
             jax.ShapeDtypeStruct((128, 2048), BF),
             jax.ShapeDtypeStruct((128, 2048), BF),
             jax.ShapeDtypeStruct((128, 2048), BF),
@@ -528,7 +602,7 @@
             jax.ShapeDtypeStruct((4, 32, 2048), BF),
         ),
         in_specs=[anywhere] * 10,
-        out_specs=[pl.BlockSpec(memory_space=pltpu.VMEM)] * 5,
+        out_specs=[anywhere] * 6,
         scratch_shapes=scratch,
         compiler_params=pltpu.CompilerParams(
             collective_id=0, has_side_effects=True, vmem_limit_bytes=58 << 20
@@ -537,18 +611,26 @@
         queries[0], key_proj[0], value_proj[0], filters.reshape(16, 128, 128), out_weight,
         out_grad[0], *tables,
     )
-    wide = mixed.astype(F32)
-    key_grad = (wide * value_proj[0].astype(F32)).astype(BF)
-    value_grad = (wide * key_proj[0].astype(F32)).astype(BF)
-    scale = 1.0 / math.sqrt(16384.0)
-    return (
-        block[None],
-        query[None],
-        key_grad[None],
-        value_grad[None],
-        filt.astype(F32).reshape(2048, 128) * scale,
-        weight.astype(F32).reshape(128, 2048) * scale,
-    )
+    block, query, key, value, filt, weight = pl.pallas_call(
+        finish,
+        name="finish",
+        out_shape=(
+            jax.ShapeDtypeStruct((128, 2048), BF),
+            jax.ShapeDtypeStruct((128, 2048), BF),
+            jax.ShapeDtypeStruct((128, 2048), BF),
+            jax.ShapeDtypeStruct((128, 2048), BF),
+            jax.ShapeDtypeStruct((2048, 128), F32),
+            jax.ShapeDtypeStruct((128, 2048), F32),
+        ),
+        in_specs=[anywhere] * 6,
+        out_specs=[anywhere] * 6,
+        scratch_shapes=[
+            vm((2048, 128), BF), vm((128, 2048), BF), vm((2048, 128), F32), vm((128, 2048), F32),
+            vm((4, 128, 2048), BF), dma((12,)),
+        ],
+        compiler_params=pltpu.CompilerParams(vmem_limit_bytes=58 << 20),
+    )(block, query, key, value, filt.reshape(2048, 128), weight.reshape(128, 2048))
+    return block[None], query[None], key[None], value[None], filt, weight
 
 
 def solution(mesh):

time: 88.8 us -> 84.8 us (0.955)
  other arithmetic: 4.57 us -> 0 us
  Pallas kernels: 81.7 us -> 83.6 us
  local copies, waits for them, and re-layouts: 1.61 us -> 0 us
    pallas_call x0 -> x1, Pallas kernels: none -> 3.22 us  [shards(): pl.pallas_call(finish, name='finish', out_shape=(jax.ShapeDtypeStruct((12...]
    broadcast_in_dim x1 -> x0, other arithmetic: 2.41 us -> none  [shards(): value_grad[None]]
    mul x2 -> x0, other arithmetic: 2.16 us -> none  [the longest x1 1.08 us: shards(): filt.astype(F32).reshape(2048, 128) * scale]
    unnamed x14 -> x0, local copies, waits for them, and re-layouts: 1.61 us -> none
    pallas_call x1, Pallas kernels: 81.7 us -> 80.4 us  [shards(): pl.pallas_call(kernel, name='hyena_block', out_shape=(jax.ShapeDtypeStruc...]
where the time goes in v2:
time: 84.8 us; the launch traced here: 84.3 us
  Pallas kernels  83.6 us (99%)
    pallas_call x1, Pallas kernels, shards(): pl.pallas_call(kernel, name='hyena_block', out_shape=(jax.ShapeDtypeStruc...  80.4 us
    pallas_call x1, Pallas kernels, shards(): pl.pallas_call(finish, name='finish', out_shape=(jax.ShapeDtypeStruct((12...  3.22 us

profile of v2, /device:TPU:2, one launch (start us, length us, event | category | flops | bytes accessed | tf_op | source)
XLA Modules:
  0.0 84.3 jit_solution(6702150076247735425)
XLA Ops:
  0.6 80.4 %hyena_block.1 = (bf16[128,2048]{1,0:T(8,128)(2,1)}, bf16[128,2048]{1,0:T(8,128)(2,1)}, bf16[128,2048]{1,0:T(8,128)(2,1)}, bf16[128,2048]{1,0:T(8,128)(2,1)}, bf...) custom-call(bf16[128,2048]{1,0:T(8,128)(2,1)} %bitcast.12, bf16[128,2048]{1,0:T(8,128)(2,1)} %bitcast.13, ...), custom_call_target="tpu_custom_call" | custom-call | tf_op jit(solution)/shard_map/hyena_block/pallas_call | solution.py:593
  81.0 3.2 %finish.1 = (bf16[128,2048]{1,0:T(8,128)(2,1)}, bf16[128,2048]{1,0:T(8,128)(2,1)}, bf16[128,2048]{1,0:T(8,128)(2,1)}, bf16[128,2048]{1,0:T(8,128)(2,1)}, f32[2048,128]{1,0:T(8,128)}, /*index=5*/f32[128,2048]{1,0:T(8,128)}) custom-call(bf16[128,2048]{1,0:T(8,128)(2,1)} %get-tuple-element.18.block_in, bf16[128,2048]{1,0:T(8,128)(2,1)} %get-tuple-element.19.query_in, ...), custom_call_target="tpu_custom_call" | custom-call | tf_op jit(solution)/shard_map/finish/pallas_call | solution.py:614

commit v3 on v2

--- a/solution.py
+++ b/solution.py
@@ -12,6 +12,8 @@
 MESH = pl.DeviceIdType.MESH
 BF = jnp.bfloat16
 F32 = jnp.float32
+
+COLS_W = 768
 
 
 def make_tables():
@@ -139,22 +141,25 @@
         return remote(ref, ref, g_s.at[4 + at], g_r.at[4 + at], dp, i * 4 + j_core)
 
     def w_copy(at):
-        rows = pl.ds(0, 64)
-        return remote(
-            w_in.at[rows], w_tile.at[i, rows], w_s.at[at], w_r.at[at], dp, i_peer(at) * 4 + j
-        )
-
-    def w_rows():
-        return pl.ds(pl.multiple_of(64 + z * 16, 16), 16)
+        cols = pl.ds(0, COLS_W)
+        return remote(
+            w_in.at[:, cols], w_tile.at[i, :, cols], w_s.at[at], w_r.at[at],
+            dp, i_peer(at) * 4 + j,
+        )
+
+    def w_part():
+        return pl.ds(pl.multiple_of(z * 32, 32), 32), pl.ds(COLS_W, 2048 - COLS_W)
 
     def wq_copy(at):
-        return remote(
-            w_in.at[w_rows()], w_tile.at[i, w_rows()], wq_s.at[at], wq_r.at[at],
+        rows, cols = w_part()
+        return remote(
+            w_in.at[rows, cols], w_tile.at[i, rows, cols], wq_s.at[at], wq_r.at[at],
             dp, i_peer(at) * 4 + j,
         )
 
     def wf_copy(at):
-        ref = w_tile.at[i_peer(1 + lax.rem(at, 3)), w_rows()]
+        rows, cols = w_part()
+        ref = w_tile.at[i_peer(1 + lax.rem(at, 3)), rows, cols]
         return remote(ref, ref, wf_s.at[at], wf_r.at[at], to_z(1 + lax.div(at, 3)), me)
 
     def conv_copy(at):
@@ -268,8 +273,8 @@
         q_send[p % 4, p // 4] = q_v[:, p * 128 : p * 128 + 128]
 
     pl.semaphore_wait(barrier, 19)
+    each(wq_copy, 4, "start")
     each(mixed_copy, 16, "start")
-    each(wq_copy, 4, "start")
     mixed_recv[me] = mixed_send[me]
     q_tile[:, j] = q_send[j]
 
@@ -383,9 +388,8 @@
         y = dot(gated_t[...], g_tile[:, :, cols].reshape(512, 256))
         out[:, :, lanes] = y.astype(BF).reshape(4, 128, 256)
 
-    loop(4, lambda n: wg_step(wga_send, n, 0))
-    each(wga_copy, 4, "start")
-    loop(4, lambda n: wg_step(wgb_send, n, 1024))
+    loop(5, lambda n: wg_step(wga_send, n, 0))
+    loop(3, lambda n: wg_step(wgb_send, n, 1280))
     each(wgb_copy, 4, "start")
 
     block_near(1 - far).wait_recv()
@@ -401,6 +405,7 @@
 
     each(cg_mine, 4, "wait_recv")
     each(cg_other, 4, "wait_recv")
+    each(wga_copy, 4, "start")
     outer_step(cg_recv)
 
     def back_step(k0):
@@ -428,27 +433,6 @@
         q_v[:, p * 128 : p * 128 + 128] = qg_recv[p % 4, p // 4]
     leave(0, q_v, query_out).start()
 
-    each(wga_copy, 4, "wait_recv")
-
-    def suma_step(r):
-        total = wga_send[i, rows16(r), :].astype(F32)
-        for at in range(1, 4):
-            total += wga_recv[at, rows16(r), :].astype(F32)
-        wsa_send[lax.div(r, 2), rows16(lax.rem(r, 2)), :] = total.astype(BF)
-
-    loop(8, suma_step)
-    each(wsa_copy, 4, "start")
-    each(wgb_copy, 4, "wait_recv")
-
-    def sumb_step(r):
-        total = wgb_send[r, pl.ds(pl.multiple_of(z * 32, 32), 32), :].astype(F32)
-        for at in range(1, 4):
-            total += wgb_recv[at, r].astype(F32)
-        wsb_send[r] = total.astype(BF)
-
-    loop(4, sumb_step)
-    each(wsb_copy, 4, "start")
-
     each(f_copy, 4, "wait_recv")
     total = f_send[z].astype(F32)
     for at in range(1, 4):
@@ -456,21 +440,42 @@
     fx_send[...] = total.astype(BF)
     fx_copy(0).start()
 
+    each(wga_copy, 4, "wait_recv")
+
+    def suma_step(r):
+        total = wga_send[i, rows16(r), :].astype(F32)
+        for at in range(1, 4):
+            total += wga_recv[at, rows16(r), :].astype(F32)
+        wsa_send[lax.div(r, 2), rows16(lax.rem(r, 2)), :] = total.astype(BF)
+
+    loop(8, suma_step)
+    each(wsa_copy, 4, "start")
+    each(wgb_copy, 4, "wait_recv")
+
+    def sumb_step(r):
+        total = wgb_send[r, pl.ds(pl.multiple_of(z * 32, 32), 32), :].astype(F32)
+        for at in range(1, 4):
+            total += wgb_recv[at, r].astype(F32)
+        wsb_send[r] = total.astype(BF)
+
+    loop(4, sumb_step)
+    each(wsb_copy, 4, "start")
+
+    fx_copy(0).wait_recv()
+    f_total[z] = (fx_send[...].astype(F32) + fx_recv[...].astype(F32)).astype(BF)
+    each(fa_copy, 4, "start")
+
     each(wsa_copy, 4, "wait_recv")
     total = wsa_send[z].astype(F32)
     for at in range(1, 4):
         total += wsa_recv[at].astype(F32)
-    wx_send[:, :1024] = total.astype(BF)
+    wx_send[:, :1280] = total.astype(BF)
     each(wsb_copy, 4, "wait_recv")
     total = wsb_send[i].astype(F32)
     for at in range(1, 4):
         total += wsb_recv[at].astype(F32)
-    wx_send[:, 1024:] = total.astype(BF)
+    wx_send[:, 1280:] = total.astype(BF)
     wx_copy(0).start()
-
-    fx_copy(0).wait_recv()
-    f_total[z] = (fx_send[...].astype(F32) + fx_recv[...].astype(F32)).astype(BF)
-    each(fa_copy, 4, "start")
 
     block_near(far).wait_recv()
     block_cross(0).wait_recv()
@@ -573,10 +578,10 @@
         vm((4, 4, 128, 128), BF), vm((4, 4, 128, 128), BF),
         vm((4, 128, 2048), BF), vm((2, 128, 2048), BF),
         vm((128, 2048), BF), vm((128, 2048), BF),
-        vm((4, 128, 1024), BF), vm((4, 128, 1024), BF),
-        vm((4, 128, 1024), BF), vm((4, 4, 32, 1024), BF),
-        vm((4, 32, 1024), BF), vm((4, 32, 1024), BF),
-        vm((4, 32, 1024), BF), vm((4, 32, 1024), BF),
+        vm((4, 128, 1280), BF), vm((4, 128, 1280), BF),
+        vm((4, 128, 768), BF), vm((4, 4, 32, 768), BF),
+        vm((4, 32, 1280), BF), vm((4, 32, 1280), BF),
+        vm((4, 32, 768), BF), vm((4, 32, 768), BF),
         vm((32, 2048), BF), vm((32, 2048), BF),
         vm((16, 128, 128), BF), vm((16, 128, 128), BF),
         vm((4, 4, 128, 128), BF), vm((4, 4, 128, 128), BF),

time: 84.8 us -> 84.3 us (level)
  no operation moved by 1% of the time
where the time goes in v3:
time: 84.3 us; the launch traced here: 84.1 us
  Pallas kernels  83.5 us (99%)
    pallas_call x1, Pallas kernels, shards(): pl.pallas_call(kernel, name='hyena_block', out_shape=(jax.ShapeDtypeStruc...  80.3 us
    pallas_call x1, Pallas kernels, shards(): pl.pallas_call(finish, name='finish', out_shape=(jax.ShapeDtypeStruct((12...  3.22 us

profile of v3, /device:TPU:2, one launch (start us, length us, event | category | flops | bytes accessed | tf_op | source)
XLA Modules:
  0.0 84.1 jit_solution(10851701391429194252)
XLA Ops:
  0.6 80.3 %hyena_block.1 = (bf16[128,2048]{1,0:T(8,128)(2,1)}, bf16[128,2048]{1,0:T(8,128)(2,1)}, bf16[128,2048]{1,0:T(8,128)(2,1)}, bf16[128,2048]{1,0:T(8,128)(2,1)}, bf...) custom-call(bf16[128,2048]{1,0:T(8,128)(2,1)} %bitcast.12, bf16[128,2048]{1,0:T(8,128)(2,1)} %bitcast.13, ...), custom_call_target="tpu_custom_call" | custom-call | tf_op jit(solution)/shard_map/hyena_block/pallas_call | solution.py:598
  80.9 3.2 %finish.1 = (bf16[128,2048]{1,0:T(8,128)(2,1)}, bf16[128,2048]{1,0:T(8,128)(2,1)}, bf16[128,2048]{1,0:T(8,128)(2,1)}, bf16[128,2048]{1,0:T(8,128)(2,1)}, f32[2048,128]{1,0:T(8,128)}, /*index=5*/f32[128,2048]{1,0:T(8,128)}) custom-call(bf16[128,2048]{1,0:T(8,128)(2,1)} %get-tuple-element.18.block_in, bf16[128,2048]{1,0:T(8,128)(2,1)} %get-tuple-element.19.query_in, ...), custom_call_target="tpu_custom_call" | custom-call | tf_op jit(solution)/shard_map/finish/pallas_call | solution.py:619

commit v4 on v3

--- a/solution.py
+++ b/solution.py
@@ -503,15 +503,11 @@
     leave(2, key_v, key_out).start()
     leave(5, value_v, value_out).start()
 
-    each(fa_copy, 4, "wait_recv")
-    leave(3, f_total, filter_out).start()
-    each(wa_copy, 4, "wait_recv")
-    leave(4, w_total, weight_out).start()
     each(mixed_copy, 16, "wait_send")
     each(mg_copy, 16, "wait_send")
     for copy in (
         q_copy, w_copy, wq_copy, conv_copy, cg_mine, cg_other, qg_copy, wga_copy, wgb_copy, wsa_copy,
-        wsb_copy, wa_copy, f_copy, fa_copy,
+        wsb_copy, f_copy,
     ):
         each(copy, 4, "wait_send")
     loop(9, lambda at: wf_copy(at).wait_send())
@@ -520,6 +516,12 @@
             copy(at).wait_send()
     for copy in (block_cross, wx_copy, fx_copy):
         copy(0).wait_send()
+    each(fa_copy, 4, "wait_recv")
+    leave(3, f_total, filter_out).start()
+    each(wa_copy, 4, "wait_recv")
+    leave(4, w_total, weight_out).start()
+    each(fa_copy, 4, "wait_send")
+    each(wa_copy, 4, "wait_send")
     for at, (src, dst) in enumerate(
         [(q_v, query_out), (block_v, block_out), (key_v, key_out), (f_total, filter_out),
          (w_total, weight_out), (value_v, value_out)]

time: 84.3 us -> 84.3 us (level)
  no operation moved by 1% of the time
where the time goes in v4:
time: 84.3 us; the launch traced here: 84.1 us
  Pallas kernels  83.5 us (99%)
    pallas_call x1, Pallas kernels, shards(): pl.pallas_call(kernel, name='hyena_block', out_shape=(jax.ShapeDtypeStruc...  80.3 us
    pallas_call x1, Pallas kernels, shards(): pl.pallas_call(finish, name='finish', out_shape=(jax.ShapeDtypeStruct((12...  3.22 us

profile of v4, /device:TPU:2, one launch (start us, length us, event | category | flops | bytes accessed | tf_op | source)
XLA Modules:
  0.0 84.1 jit_solution(3984006418332069754)
XLA Ops:
  0.6 80.3 %hyena_block.1 = (bf16[128,2048]{1,0:T(8,128)(2,1)}, bf16[128,2048]{1,0:T(8,128)(2,1)}, bf16[128,2048]{1,0:T(8,128)(2,1)}, bf16[128,2048]{1,0:T(8,128)(2,1)}, bf...) custom-call(bf16[128,2048]{1,0:T(8,128)(2,1)} %bitcast.12, bf16[128,2048]{1,0:T(8,128)(2,1)} %bitcast.13, ...), custom_call_target="tpu_custom_call" | custom-call | tf_op jit(solution)/shard_map/hyena_block/pallas_call | solution.py:600
  80.9 3.2 %finish.1 = (bf16[128,2048]{1,0:T(8,128)(2,1)}, bf16[128,2048]{1,0:T(8,128)(2,1)}, bf16[128,2048]{1,0:T(8,128)(2,1)}, bf16[128,2048]{1,0:T(8,128)(2,1)}, f32[2048,128]{1,0:T(8,128)}, /*index=5*/f32[128,2048]{1,0:T(8,128)}) custom-call(bf16[128,2048]{1,0:T(8,128)(2,1)} %get-tuple-element.18.block_in, bf16[128,2048]{1,0:T(8,128)(2,1)} %get-tuple-element.19.query_in, ...), custom_call_target="tpu_custom_call" | custom-call | tf_op jit(solution)/shard_map/finish/pallas_call | solution.py:621
